TPU v7x, 32 devices: a whole 2x2x4 slice. The times are simulated.
32 devices in a mesh: grp: 2 (over x), head: 16 (over z, y, core).
Axes of the slice: x: 2, y: 2, z: 4, core: 2. Of those that a mesh axis runs over, the one named last changes fastest.
Arguments:
- query: bfloat16 [72, 256, 2048], P('grp', 'head'), may hold values from -24 to 24
- out_grad: bfloat16 [72, 256, 2048], P('grp', 'head'), may hold values from -6 to 6
- forward_out: bfloat16 [72, 256, 2048], P('grp', 'head'), may hold values from -6 to 6
- key_codes: bfloat16 [4, 256, 2048], P('grp', 'head'), may hold values from -127 to 127, as said below
- key_scale: bfloat16 [4, 256, 16], P('grp', 'head'), may hold values from 0.0039 to 0.0402
- value_codes: bfloat16 [4, 256, 2048], P('grp', 'head'), may hold values from -127 to 127, as said below
- value_scale: bfloat16 [4, 256, 16], P('grp', 'head'), may hold values from 0.0039 to 0.0402
- pairing: int32 [72, 2], replicated, may hold values from 0 to 3, as said below
Outputs:
- grad_query: bfloat16 [72, 256, 2048], P('grp', 'head')
- grad_key: bfloat16 [4, 256, 2048], P('grp', 'head')
- grad_value: bfloat16 [4, 256, 2048], P('grp', 'head')
Inputs may be any that keep to these rules, and one draw needn't show every extreme that they name: `key_codes`: whole numbers. `value_codes`: whole numbers. `pairing`: the two entries of a row differ.
All inputs are finite; a program needn't handle non-finite values.
Results may differ from a plain program's by a relative error of at most 0.012.
The roundings to bfloat16 on the way count: a program that leaves them out, or rounds other values in their place, can miss the bound.
Values may be sent and summed in bfloat16 or wider, within the bound.
A program may use at most 192 MiB of HBM per device.

v0:
```python
import functools
import math

import jax
import jax.numpy as jnp
from jax import lax
from jax.experimental import pallas as pl
from jax.experimental.pallas import tpu as pltpu
from jax.sharding import Mesh, PartitionSpec as P

HD = 128
SCALE = HD ** -0.5
ROWS = 256
NT = (((1,), (1,)), ((), ()))
NN = (((1,), (0,)), ((), ()))


def dot(a, b, dims):
    return lax.dot_general(a, b, dims, preferred_element_type=jnp.float32)


def grads_kernel(
    core_ref, bias_ref, q_own, g_own, o_own, swapped, k_ref, v_ref,
    dq_own, dq_in, dk_ref, dv_ref, q_all, g_all, dots, dq_all, dk_acc, dv_acc,
):
    own = q_own.shape[0]
    rows = 2 * own
    keys = k_ref.shape[0]
    q_all[:own] = q_own[...]
    q_all[own:] = swapped[0]
    g_all[:own] = g_own[...]
    g_all[own:] = swapped[1]
    ones = jnp.ones((8, HD), jnp.bfloat16)
    for part, (grad, out) in enumerate(((g_own[...], o_own[...]), (swapped[1], swapped[2]))):
        product = grad.astype(jnp.float32) * out.astype(jnp.float32)
        high = product.astype(jnp.bfloat16)
        low = (product - high.astype(jnp.float32)).astype(jnp.bfloat16)
        dots[:, part * own:(part + 1) * own] = dot(ones, high, NT) + dot(ones, low, NT)
    k_all = k_ref[...]
    v_all = v_ref[...]
    k_turned = k_all.astype(jnp.float32).T.astype(jnp.bfloat16)
    dk_acc[...] = jnp.zeros_like(dk_acc)
    dv_acc[...] = jnp.zeros_like(dv_acc)
    for start in range(0, rows, ROWS):
        size = min(ROWS, rows - start)
        at = pl.ds(start, size)
        q = q_all[at, :]
        g = g_all[at, :]
        bias = bias_ref[:, :, :, :, at]
        scores = dot(k_all, q, NT)
        span = keys // (bias.shape[0] * bias.shape[1] * bias.shape[2])
        masked = scores.reshape(bias.shape[:3] + (span, size)) + bias
        masked = masked.reshape(keys, size)
        highest = jnp.max(masked, axis=0, keepdims=True)
        weights = jnp.exp2((masked - highest) * (SCALE * math.log2(math.e)))
        probs = weights * (1.0 / jnp.sum(weights, axis=0, keepdims=True))
        dv_acc[...] += dot(probs.astype(jnp.bfloat16), g, NN)
        prob_grad = dot(v_all, g, NT)
        score_grad = (probs * (prob_grad - dots[0:1, at]) * SCALE).astype(jnp.bfloat16)
        dk_acc[...] += dot(score_grad, q, NN)
        dq_all[at, :] = dot(k_turned, score_grad, NN).T.astype(jnp.bfloat16)
    dq_own[...] = dq_all[:own]
    dq_in[...] = dq_all[own:]
    dk_ref[...] = dk_acc[...].astype(jnp.bfloat16)
    dv_ref[...] = dv_acc[...].astype(jnp.bfloat16)


def local_grads(core, bias, q, g, o, swapped, keys, values):
    own, half = q.shape[0], q.shape[1] // 2
    heads = half // HD
    count = keys.shape[0]
    offset = (core * heads).reshape(1).astype(jnp.int32)
    mine = pl.BlockSpec((own, HD), lambda h, c: (0, c[0] + h))
    column = pl.BlockSpec((own, HD), lambda h, c: (0, h))
    table = pl.BlockSpec((count, HD), lambda h, c: (0, h))
    return pl.pallas_call(
        grads_kernel,
        grid_spec=pltpu.PrefetchScalarGridSpec(
            num_scalar_prefetch=1,
            grid=(heads,),
            in_specs=[
                pl.BlockSpec(bias.shape, lambda h, c: (0, 0, 0, 0, 0)),
                mine, mine, mine,
                pl.BlockSpec((3, own, HD), lambda h, c: (0, 0, h)),
                table, table,
            ],
            out_specs=[column, column, table, table],
            scratch_shapes=[
                pltpu.VMEM((2 * own, HD), jnp.bfloat16),
                pltpu.VMEM((2 * own, HD), jnp.bfloat16),
                pltpu.VMEM((8, 2 * own), jnp.float32),
                pltpu.VMEM((2 * own, HD), jnp.bfloat16),
                pltpu.VMEM((count, HD), jnp.float32),
                pltpu.VMEM((count, HD), jnp.float32),
            ],
        ),
        out_shape=[
            jax.ShapeDtypeStruct((own, half), jnp.bfloat16),
            jax.ShapeDtypeStruct((own, half), jnp.bfloat16),
            jax.ShapeDtypeStruct((count, half), jnp.bfloat16),
            jax.ShapeDtypeStruct((count, half), jnp.bfloat16),
        ],
        compiler_params=pltpu.CompilerParams(vmem_limit_bytes=40 * 2 ** 20),
        cost_estimate=pl.CostEstimate(
            flops=20 * own * count * half, bytes_accessed=14 * own * half + 8 * count * half,
            transcendentals=2 * own * count * heads,
        ),
    )(offset, bias, q, g, o, swapped, keys, values)


def dequantize(codes, scales):
    count, length, width = codes.shape
    heads = scales.shape[2]
    values = (
        codes.astype(jnp.float32).reshape(count, length, heads, width // heads)
        * scales.astype(jnp.float32)[..., None]
    )
    return values.reshape(count, length, width).astype(jnp.bfloat16)


def swap(array):
    return lax.ppermute(array, "core", [(0, 1), (1, 0)])


def in_order(core, mine, other, axis):
    return jnp.where(
        core == 0,
        jnp.concatenate([mine, other], axis=axis),
        jnp.concatenate([other, mine], axis=axis),
    )


def on_device(group_count, query, out_grad, forward_out, key_codes, key_scale, value_codes, value_scale, pairing):
    core = lax.axis_index("core")
    group = lax.axis_index("grp")
    blocks, tokens, width = query.shape
    half = width // 2
    own = blocks * tokens
    table = jnp.stack([dequantize(key_codes, key_scale), dequantize(value_codes, value_scale)])
    kept = lax.dynamic_slice_in_dim(table, core * half, half, axis=3)
    other = swap(lax.dynamic_slice_in_dim(table, (1 - core) * half, half, axis=3))
    shard = in_order(core, kept, other, 2)
    kv_local, kv_tokens = shard.shape[1:3]
    gathered = [
        lax.all_gather(shard[i].reshape(kv_local * kv_tokens, half), ("grp", "chip"), axis=0, tiled=True)
        for i in range(2)
    ]
    flat = [a.reshape(own, width) for a in (query, out_grad, forward_out)]
    swapped = swap(jnp.stack([
        lax.dynamic_slice_in_dim(a, (1 - core) * half, half, axis=1) for a in flat
    ]))
    chips = gathered[0].shape[0] // (group_count * kv_local * kv_tokens)
    chosen = lax.dynamic_slice_in_dim(pairing, group * blocks, blocks, axis=0)
    hit = jnp.any(chosen[None] == jnp.arange(group_count * kv_local)[:, None, None], axis=2)
    bias = jnp.where(hit, 0.0, -jnp.inf).astype(jnp.float32)
    bias = jnp.tile(jnp.repeat(bias, tokens, axis=1), (1, 2))
    bias = bias.reshape(group_count, 1, kv_local, 1, 2 * own)
    bias = jnp.broadcast_to(bias, (group_count, chips, kv_local, 1, 2 * own))
    dq_mine, dq_other, dk, dv = local_grads(core, bias, *flat, swapped, *gathered)
    dq = in_order(core, dq_mine, swap(dq_other), 1).reshape(query.shape)
    sums = [
        lax.psum_scatter(a, ("grp", "chip"), scatter_dimension=0, tiled=True)
        .reshape(kv_local, kv_tokens, half)
        for a in (dk, dv)
    ]
    length = kv_tokens // 2
    sums = jnp.stack(sums)
    kept = lax.dynamic_slice_in_dim(sums, core * length, length, axis=2)
    other = swap(lax.dynamic_slice_in_dim(sums, (1 - core) * length, length, axis=2))
    grads = in_order(core, kept, other, 3)
    return dq, grads[0], grads[1]


def solution(mesh):
    groups, heads = mesh.shape["grp"], mesh.shape["head"]
    split = Mesh(mesh.devices.reshape(groups, heads // 2, 2), ("grp", "chip", "core"))
    spec = P("grp", ("chip", "core"), None)
    return jax.shard_map(
        functools.partial(on_device, groups),
        mesh=split,
        in_specs=(spec,) * 7 + (P(),),
        out_specs=(spec,) * 3,
        check_vma=False,
    )
```

profile of v0, /device:TPU:1, one launch (start us, length us, event | category | flops | bytes accessed | tf_op | source)
XLA Modules:
  0.0 361.2 jit_solution(82511044579547138)
XLA Ops:
  7.2 1.0 mul.46
  8.3 0.8 mul.49
  9.2 1.0 fusion
  10.2 0.1 collective-permute-start.1
  10.4 1.3 collective-permute-done.1
  11.7 0.7 fusion.7
  12.5 1.1 dynamic-slice_bitcast_fusion.2
  13.7 1.9 dynamic-slice_bitcast_fusion
  15.7 2.0 pad_maximum_fusion
  17.7 0.1 collective-permute-start
  17.8 0.1 constant_dynamic-slice_fusion
  17.9 0.1 broadcast_in_dim.24
  18.0 0.1 tile.7
  18.1 0.1 broadcast_in_dim.25
  18.2 6.0 %collective-permute-done.swapped = bf16[3,576,1024]{2,1,0:T(8,128)(2,1)} collective-permute-done((bf16[3,576,1024]{2,1,0:T(8,128)(2,1)}, bf16[3,576,1024]{2,1,0:T(8,128)(2,1)}, u32[]{:S(2)}, u32[]{:S(2)}) %collective-permute-start) | collective-permute-done | bytes 3538976 | tf_op jit(solution)/shard_map/ppermute | solution.py:122
  24.2 50.7 %all-gather.3.cloned.1.call-done.k_ref = bf16[1024,1024]{1,0:T(8,128)(2,1)} async-done(((bf16[64,1024]{1,0:T(8,128)(2,1)}), bf16[1024,1024]{1,0:T(8,128)(2,1)}) %all-gather.3.cloned.1.call-update) | async-done | bytes 2097168 | tf_op jit(solution)/shard_map/all_gather | solution.py:145
  75.0 62.8 %all-gather.5.cloned.1.call-done.v_ref = bf16[1024,1024]{1,0:T(8,128)(2,1)} async-done(((bf16[64,1024]{1,0:T(8,128)(2,1)}), bf16[1024,1024]{1,0:T(8,128)(2,1)}) %all-gather.5.cloned.1.call-update) | async-done | bytes 2097168 | tf_op jit(solution)/shard_map/all_gather | solution.py:145
  137.7 0.1 broadcast_in_dim.26.bias_ref
  137.8 1.6 copy-done.2
  139.4 1.6 copy-done.3
  141.0 48.0 %shard_map.103 = (bf16[576,1024]{1,0:T(8,128)(2,1)S(1)}, bf16[576,1024]{1,0:T(8,128)(2,1)S(1)}, bf16[1024,1024]{1,0:T(8,128)(2,1)}, bf16[1024,1024]{1,0:T(8,128)(2,1)}) custom-call(s32[1]{0:T(128)} %bitcast.core_ref, f32[2,8,2,1,1152]{4,3,2,1,0:T(1,128)S(1)} %broadcast_in_dim.26.bias_ref, bf16[576,2048]{1,0:T(8,128)(2,1)S(1)} %bitcast.30, ...), custom_call_target="tpu_custom_call" | custom-call | flops 12079595520 | bytes 16646144 | tf_op jit(solution)/shard_map/pallas_call | solution.py:76
  188.9 1.0 copy-done.4
  190.1 0.5 reduce-scatter.5.cloned.1.call-update
  190.6 0.7 copy-done.5
  191.2 1.1 collective-permute-start.2
  192.4 66.9 %reduce-scatter.3.cloned.1.call-done = bf16[64,1024]{1,0:T(8,128)(2,1)} async-done(((bf16[1024,1024]{1,0:T(8,128)(2,1)}), bf16[64,1024]{1,0:T(8,128)(2,1)}) %reduce-scatter.3.cloned.1.call-update) | async-done | bytes 131088 | tf_op jit(solution)/shard_map/reduce_scatter | solution.py:162
  259.3 80.0 %reduce-scatter.5.cloned.1.call-done = bf16[64,1024]{1,0:T(8,128)(2,1)} async-done(((bf16[1024,1024]{1,0:T(8,128)(2,1)}), bf16[64,1024]{1,0:T(8,128)(2,1)}) %reduce-scatter.5.cloned.1.call-update) | async-done | bytes 131088 | tf_op jit(solution)/shard_map/reduce_scatter | solution.py:162
  339.2 1.0 fusion.3
  340.2 11.8 %collective-permute-start.3 = (bf16[2,2,16,1024]{3,2,1,0:T(8,128)(2,1)S(1)}, bf16[2,2,16,1024]{3,2,1,0:T(8,128)(2,1)S(1)}, u32[]{:S(2)}, u32[]{:S(2)}) collective-permute-start(bf16[2,2,16,1024]{3,2,1,0:T(8,128)(2,1)S(1)} %get-tuple-element.14), channel_id=1, source_target_pairs={{0,1},{1,0},{2,3},{3,2},{4,5},{5,4},{6,7},{7,6},{8,9},{9,8},{10,11... | collective-permute-start | bytes 393224 | tf_op jit(solution)/shard_map/ppermute | solution.py:122
  352.0 1.9 maximum_select_fusion
  353.9 0.1 maximum_select_fusion.2
  354.0 0.7 slice_bitcast_fusion
  (26 shorter events, 0.5 us)
Async XLA Ops:
  7.2 10.7 %copy-start = (s32[72,2]{0,1:T(2,128)S(1)}, s32[72,2]{0,1:T(2,128)}, u32[]{:S(2)}) copy-start(s32[72,2]{0,1:T(2,128)} %param.15) | copy-start | bytes 1732
  7.2 5.3 %copy-start.1 = (bf16[36,16,2048]{2,1,0:T(8,128)(2,1)S(1)}, bf16[36,16,2048]{2,1,0:T(8,128)(2,1)}, u32[]{:S(2)}) copy-start(bf16[36,16,2048]{2,1,0:T(8,128)(2,1)} %param.8) | copy-start | bytes 7077892
  7.2 67.8 %all-gather.3.cloned.1.call-start = ((), (), s32[]{:S(2)}) async-start(), calls=%async_computation.2 | async-start | bytes 2228224 | tf_op jit(solution)/shard_map/all_gather | solution.py:145
  10.2 1.4 collective-permute-start.1
  12.4 125.3 %all-gather.5.cloned.1.call-start = ((), (), s32[]{:S(2)}) async-start(), calls=%async_computation.3 | async-start | bytes 2228224 | tf_op jit(solution)/shard_map/all_gather | solution.py:145
  13.7 245.6 %reduce-scatter.3.cloned.1.call-start = ((), (), s32[]{:S(2)}) async-start(), calls=%async_computation.4 | async-start | bytes 2228224 | tf_op jit(solution)/shard_map/reduce_scatter | solution.py:162
  13.7 2.0 copy-start.6
  17.7 6.6 %collective-permute-start = (bf16[3,576,1024]{2,1,0:T(8,128)(2,1)}, bf16[3,576,1024]{2,1,0:T(8,128)(2,1)}, u32[]{:S(2)}, u32[]{:S(2)}) collective-permute-start(bf16[3,576,1024]{2,1,0:T(8,128)(2,1)} %pad_maximum_fusion), channel_id=1, source_target_pairs={{0,1},{1,0},{2,3},{3,2},{4,5},{5,4},{6,7},{7,6},{8,9},{9,8},{10,11... | collective-permute-start | bytes 10616840 | tf_op jit(solution)/shard_map/ppermute | solution.py:122
  137.8 1.6 copy-start.2
  139.4 1.6 copy-start.3
  188.9 1.0 copy-start.4
  190.0 1.3 copy-start.5
  190.0 149.2 %reduce-scatter.5.cloned.1.call-start = ((), (), s32[]{:S(2)}) async-start(), calls=%async_computation.5 | async-start | bytes 2228224 | tf_op jit(solution)/shard_map/reduce_scatter | solution.py:162
  191.2 160.7 %collective-permute-start.2 = (bf16[576,1024]{1,0:T(8,128)(2,1)S(1)}, bf16[576,1024]{1,0:T(8,128)(2,1)S(1)}, u32[]{:S(2)}, u32[]{:S(2)}) collective-permute-start(bf16[576,1024]{1,0:T(8,128)(2,1)S(1)} %copy-done.5), channel_id=1, source_target_pairs={{0,1},{1,0},{2,3},{3,2},{4,5},{5,4},{6,7},{7,6},{8,9},{9,8},{10,11... | collective-permute-start | bytes 3538952 | tf_op jit(solution)/shard_map/ppermute | solution.py:122
  340.2 13.7 %collective-permute-start.3 = (bf16[2,2,16,1024]{3,2,1,0:T(8,128)(2,1)S(1)}, bf16[2,2,16,1024]{3,2,1,0:T(8,128)(2,1)S(1)}, u32[]{:S(2)}, u32[]{:S(2)}) collective-permute-start(bf16[2,2,16,1024]{3,2,1,0:T(8,128)(2,1)S(1)} %get-tuple-element.14), channel_id=1, source_target_pairs={{0,1},{1,0},{2,3},{3,2},{4,5},{5,4},{6,7},{7,6},{8,9},{9,8},{10,11... | collective-permute-start | bytes 393224 | tf_op jit(solution)/shard_map/ppermute | solution.py:122
Sparse Core Ops, SparseCore 0:
  12.6 62.3 all-gather.2
  78.3 59.3 all-gather.4
  190.1 69.1 reduce-scatter.2
  261.4 77.7 reduce-scatter.4
where the time goes:
time: 362 us; the launch traced here: 361 us
  waiting for transfers between devices  268 us (74%)
  Pallas kernels  48 us (13%)
  between operations  13.9 us (4%)
  starting transfers between devices  13.4 us (4%)
  local copies, waits for them, and re-layouts  11.7 us (3%)
  other arithmetic  6.06 us (2%)
    reduce_scatter x2, waiting for transfers between devices, on_device(): lax.psum_scatter(a, ('grp', 'chip'), scatter_dimension=0, tiled=True)  147 us
    all_gather x2, waiting for transfers between devices, on_device(): lax.all_gather(shard[i].reshape(kv_local * kv_tokens, half), ('grp', 'chi...  113 us
    pallas_call x1, Pallas kernels, local_grads(): pl.pallas_call(grads_kernel, grid_spec=pltpu.PrefetchScalarGridSpec(num_s...  48 us
    ppermute x4, starting transfers between devices, swap(): return lax.ppermute(array, 'core', [(0, 1), (1, 0)])  13.2 us
    ppermute x4, waiting for transfers between devices, swap(): return lax.ppermute(array, 'core', [(0, 1), (1, 0)])  7.31 us
  transfers between devices with their start and end apart: 8, of which 6 were waited for; matrix products, arithmetic and copies ran while one was open for 2% of the time, Pallas kernels for 0%

commit v1 on v0

--- a/solution.py
+++ b/solution.py
@@ -108,6 +108,250 @@
     )(offset, bias, q, g, o, swapped, keys, values)
 
 
+MESH = pl.DeviceIdType.MESH
+
+
+def place():
+    group, chip, core = (lax.axis_index(name) for name in ("grp", "chip", "core"))
+    line, pair = chip // 2, chip % 2
+    beside = ((1 - group, chip, core), (group, line * 2 + 1 - pair, core))
+    return group, line, pair, beside, lambda at: (group, at * 2 + pair, core)
+
+
+def meet(lines, line, beside, along):
+    barrier = pltpu.get_barrier_semaphore()
+    for device in beside:
+        pl.semaphore_signal(barrier, inc=1, device_id=device, device_id_type=MESH)
+    for side in (-1, 1):
+        @pl.when((line + side >= 0) & (line + side < lines))
+        def _():
+            pl.semaphore_signal(barrier, inc=1, device_id=along(line + side), device_id_type=MESH)
+    count = 2 + (line > 0).astype(jnp.int32) + (line < lines - 1).astype(jnp.int32)
+    pl.semaphore_wait(barrier, count)
+
+
+def remote(src, dst, send, recv, device):
+    return pltpu.make_async_remote_copy(
+        src_ref=src, dst_ref=dst, send_sem=send, recv_sem=recv, device_id=device, device_id_type=MESH
+    )
+
+
+def each(lines, line, distance, body):
+    for side in ((-1, 1) if distance else (0,)):
+        at = line + side * distance
+        if distance:
+            @pl.when((at >= 0) & (at < lines))
+            def _():
+                body(side, at)
+        else:
+            body(side, at)
+
+
+def gather_kernel(
+    lines, k_in, v_in, k_out, v_out,
+    local_sem, z_send, z_recv, s_send, s_recv, f_send, f_recv,
+):
+    group, line, pair, beside, along = place()
+    ins, outs = (k_in, v_in), (k_out, v_out)
+    locals_ = [
+        pltpu.make_async_copy(ins[kind], outs[kind].at[group, line, pair], local_sem.at[kind])
+        for kind in range(2)
+    ]
+    for copy in locals_:
+        copy.start()
+    meet(lines, line, beside, along)
+
+    def relay(kind, side, at, first):
+        slot = outs[kind].at[group, at, pair]
+        way = (side + 1) // 2
+        return remote(
+            ins[kind] if first else slot, slot, z_send.at[kind, way, at], z_recv.at[kind, at],
+            along(line + side),
+        )
+
+    def sideways(kind, way, at, first):
+        slot = outs[kind].at[group, at, pair]
+        return remote(
+            ins[kind] if first else slot, slot, s_send.at[kind, way, at], s_recv.at[kind, way, at],
+            beside[way],
+        )
+
+    def forward(kind, at):
+        slot = outs[0].at[1 - group, at, pair] if kind == 0 else outs[1].at[group, at, 1 - pair]
+        return remote(slot, slot, f_send.at[kind, at], f_recv.at[kind, at], beside[1 - kind])
+
+    def spread(distance):
+        def body(side, at):
+            for kind in range(2):
+                if distance:
+                    relay(kind, side, at, False).wait_recv()
+                for onward in ((-1, 1) if distance == 0 else (-side,)):
+                    @pl.when((line + onward >= 0) & (line + onward < lines))
+                    def _():
+                        relay(kind, onward, at, distance == 0).start()
+                for way in (kind, 1 - kind):
+                    sideways(kind, way, at, distance == 0).start()
+        each(lines, line, distance, body)
+
+    def across(distance):
+        def body(side, at):
+            for kind in range(2):
+                sideways(kind, kind, at, False).wait_recv()
+                forward(kind, at).start()
+        each(lines, line, distance, body)
+
+    def finish(distance):
+        def body(side, at):
+            for kind in range(2):
+                sideways(kind, 1 - kind, at, False).wait_recv()
+                forward(kind, at).wait_recv()
+                forward(kind, at).wait_send()
+                for way in range(2):
+                    sideways(kind, way, at, False).wait_send()
+                for onward in ((-1, 1) if distance == 0 else (-side,)):
+                    @pl.when((line + onward >= 0) & (line + onward < lines))
+                    def _():
+                        relay(kind, onward, at, False).wait_send()
+        each(lines, line, distance, body)
+
+    spread(0)
+    for distance in range(1, lines):
+        spread(distance)
+        across(distance - 1)
+    across(lines - 1)
+    for distance in range(lines):
+        finish(distance)
+    for copy in locals_:
+        copy.wait()
+
+
+def gather(keys, values, lines):
+    shape = jax.ShapeDtypeStruct((2, lines, 2) + keys.shape, keys.dtype)
+    anywhere = pl.BlockSpec(memory_space=pl.ANY)
+    dma = pltpu.SemaphoreType.DMA
+    return pl.pallas_call(
+        functools.partial(gather_kernel, lines),
+        in_specs=[anywhere] * 2,
+        out_specs=[anywhere] * 2,
+        out_shape=[shape] * 2,
+        scratch_shapes=[
+            dma((2,)), dma((2, 2, lines)), dma((2, lines)), dma((2, 2, lines)), dma((2, 2, lines)),
+            dma((2, lines)), dma((2, lines)),
+        ],
+        compiler_params=pltpu.CompilerParams(collective_id=0, has_side_effects=True),
+    )(keys, values)
+
+
+def scatter_kernel(
+    lines, k_ref, v_ref, out_ref, first_in, second_out, second_in, line_out, line_in, total,
+    a_send, a_recv, b_send, b_recv, z_send, z_recv,
+):
+    group, line, pair, beside, along = place()
+    refs = (k_ref, v_ref)
+    meet(lines, line, beside, along)
+
+    def first(kind, at):
+        src = k_ref.at[1 - group, at] if kind == 0 else v_ref.at[:, at, 1 - pair]
+        return remote(src, first_in.at[kind, at], a_send.at[kind, at], a_recv.at[kind, at], beside[kind])
+
+    def second(kind, at):
+        return remote(
+            second_out.at[kind, at], second_in.at[kind, at], b_send.at[kind, at], b_recv.at[kind, at],
+            beside[1 - kind],
+        )
+
+    def pass_on(kind, side, at):
+        way = (side + 1) // 2
+        return remote(
+            line_out.at[kind, at], line_in.at[kind, way, at], z_send.at[kind, at],
+            z_recv.at[kind, way, at], along(line + side),
+        )
+
+    def start(distance):
+        def body(side, at):
+            for kind in range(2):
+                first(kind, at).start()
+        each(lines, line, distance, body)
+
+    def halve(distance):
+        def body(side, at):
+            for kind in range(2):
+                first(kind, at).wait_recv()
+                if kind == 0:
+                    mine, come = k_ref[group, at, 1 - pair], first_in[0, at, 1 - pair]
+                else:
+                    mine, come = v_ref[1 - group, at, pair], first_in[1, at, 1 - group]
+                second_out[kind, at] = (mine.astype(jnp.float32) + come.astype(jnp.float32)).astype(jnp.bfloat16)
+                second(kind, at).start()
+        each(lines, line, distance, body)
+
+    def collect(distance):
+        def body(side, at):
+            for kind in range(2):
+                second(kind, at).wait_recv()
+                come = first_in[kind, at, pair if kind == 0 else group]
+                total[kind] = (
+                    refs[kind][group, at, pair].astype(jnp.float32) + come.astype(jnp.float32)
+                    + second_in[kind, at].astype(jnp.float32)
+                )
+                for way in ((-1, 1) if distance == 0 else (side,)):
+                    @pl.when((line - way >= 0) & (line - way < lines))
+                    def _():
+                        pass_on(kind, way, at).wait_recv()
+                        total[kind] += line_in[kind, (way + 1) // 2, at].astype(jnp.float32)
+                if distance:
+                    line_out[kind, at] = total[kind].astype(jnp.bfloat16)
+                    pass_on(kind, side, at).start()
+                else:
+                    out_ref[kind] = total[kind].astype(jnp.bfloat16)
+        each(lines, line, distance, body)
+
+    def finish(distance):
+        def body(side, at):
+            for kind in range(2):
+                first(kind, at).wait_send()
+                second(kind, at).wait_send()
+                if distance:
+                    pass_on(kind, side, at).wait_send()
+        each(lines, line, distance, body)
+
+    order = list(range(lines - 1, -1, -1))
+    for turn in range(lines + 3):
+        if turn < lines:
+            start(order[turn])
+        if 0 <= turn - 2 < lines:
+            halve(order[turn - 2])
+        if 0 <= turn - 3 < lines:
+            collect(order[turn - 3])
+    for distance in range(lines):
+        finish(distance)
+
+
+def scatter(dk, dv):
+    lines, rows, half = dk.shape[1], dk.shape[3], dk.shape[4]
+    here = pl.BlockSpec(memory_space=pltpu.VMEM)
+    dma = pltpu.SemaphoreType.DMA
+    return pl.pallas_call(
+        functools.partial(scatter_kernel, lines),
+        in_specs=[here] * 2,
+        out_specs=here,
+        out_shape=jax.ShapeDtypeStruct((2, rows, half), jnp.bfloat16),
+        scratch_shapes=[
+            pltpu.VMEM((2, lines, 2, rows, half), jnp.bfloat16),
+            pltpu.VMEM((2, lines, rows, half), jnp.bfloat16),
+            pltpu.VMEM((2, lines, rows, half), jnp.bfloat16),
+            pltpu.VMEM((2, lines, rows, half), jnp.bfloat16),
+            pltpu.VMEM((2, 2, lines, rows, half), jnp.bfloat16),
+            pltpu.VMEM((2, rows, half), jnp.float32),
+            dma((2, lines)), dma((2, lines)), dma((2, lines)), dma((2, lines)),
+            dma((2, lines)), dma((2, 2, lines)),
+        ],
+        compiler_params=pltpu.CompilerParams(
+            collective_id=1, has_side_effects=True, vmem_limit_bytes=56 * 2 ** 20,
+        ),
+    )(dk, dv)
+
+
 def dequantize(codes, scales):
     count, length, width = codes.shape
     heads = scales.shape[2]
@@ -130,7 +374,7 @@
     )
 
 
-def on_device(group_count, query, out_grad, forward_out, key_codes, key_scale, value_codes, value_scale, pairing):
+def on_device(group_count, lines, query, out_grad, forward_out, key_codes, key_scale, value_codes, value_scale, pairing):
     core = lax.axis_index("core")
     group = lax.axis_index("grp")
     blocks, tokens, width = query.shape
@@ -141,10 +385,8 @@
     other = swap(lax.dynamic_slice_in_dim(table, (1 - core) * half, half, axis=3))
     shard = in_order(core, kept, other, 2)
     kv_local, kv_tokens = shard.shape[1:3]
-    gathered = [
-        lax.all_gather(shard[i].reshape(kv_local * kv_tokens, half), ("grp", "chip"), axis=0, tiled=True)
-        for i in range(2)
-    ]
+    shard = shard.reshape(2, kv_local * kv_tokens, half)
+    gathered = [a.reshape(-1, half) for a in gather(shard[0], shard[1], lines)]
     flat = [a.reshape(own, width) for a in (query, out_grad, forward_out)]
     swapped = swap(jnp.stack([
         lax.dynamic_slice_in_dim(a, (1 - core) * half, half, axis=1) for a in flat
@@ -158,13 +400,9 @@
     bias = jnp.broadcast_to(bias, (group_count, chips, kv_local, 1, 2 * own))
     dq_mine, dq_other, dk, dv = local_grads(core, bias, *flat, swapped, *gathered)
     dq = in_order(core, dq_mine, swap(dq_other), 1).reshape(query.shape)
-    sums = [
-        lax.psum_scatter(a, ("grp", "chip"), scatter_dimension=0, tiled=True)
-        .reshape(kv_local, kv_tokens, half)
-        for a in (dk, dv)
-    ]
+    split = (2, lines, 2, kv_local * kv_tokens, half)
+    sums = scatter(dk.reshape(split), dv.reshape(split)).reshape(2, kv_local, kv_tokens, half)
     length = kv_tokens // 2
-    sums = jnp.stack(sums)
     kept = lax.dynamic_slice_in_dim(sums, core * length, length, axis=2)
     other = swap(lax.dynamic_slice_in_dim(sums, (1 - core) * length, length, axis=2))
     grads = in_order(core, kept, other, 3)
@@ -176,7 +414,7 @@
     split = Mesh(mesh.devices.reshape(groups, heads // 2, 2), ("grp", "chip", "core"))
     spec = P("grp", ("chip", "core"), None)
     return jax.shard_map(
-        functools.partial(on_device, groups),
+        functools.partial(on_device, groups, heads // 4),
         mesh=split,
         in_specs=(spec,) * 7 + (P(),),
         out_specs=(spec,) * 3,

time: 362 us -> 161 us (0.44)
  waiting for transfers between devices: 268 us -> 5.92 us
  Pallas kernels: 48 us -> 133 us
  between operations: 13.9 us -> 0.87 us
  starting transfers between devices: 13.4 us -> 3.72 us
    reduce_scatter x2 -> x0, waiting for transfers between devices: 147 us -> none  [on_device(): lax.psum_scatter(a, ('grp', 'chip'), scatter_dimension=0, tiled=True)]
    all_gather x2 -> x0, waiting for transfers between devices: 113 us -> none  [on_device(): lax.all_gather(shard[i].reshape(kv_local * kv_tokens, half), ('grp', 'chi...]
    pallas_call x0 -> x2, Pallas kernels: none -> 84.1 us  [the longest x1 45.3 us: scatter(): pl.pallas_call(functools.partial(scatter_kernel, lines), in_specs=[here]...]
    ppermute x4, starting transfers between devices: 13.2 us -> 3.72 us  [swap(): return lax.ppermute(array, 'core', [(0, 1), (1, 0)])]
  transfers between devices with their start and end apart: 8 -> 4, of which waited for: 6 -> 2; matrix products, arithmetic and copies ran while one was open for 2% -> 2% of each run, Pallas kernels for 0% -> 53%
where the time goes in v1:
time: 161 us; the launch traced here: 160 us
  Pallas kernels  133 us (83%)
  local copies, waits for them, and re-layouts  12.6 us (8%)
  waiting for transfers between devices  5.92 us (4%)
  other arithmetic  4.18 us (3%)
  starting transfers between devices  3.72 us (2%)
    pallas_call x1, Pallas kernels, local_grads(): pl.pallas_call(grads_kernel, grid_spec=pltpu.PrefetchScalarGridSpec(num_s...  48.5 us
    pallas_call x1, Pallas kernels, scatter(): pl.pallas_call(functools.partial(scatter_kernel, lines), in_specs=[here]...  45.3 us
    pallas_call x1, Pallas kernels, gather(): pl.pallas_call(functools.partial(gather_kernel, lines), in_specs=[anywher...  38.8 us
    unnamed x22, local copies, waits for them, and re-layouts  6.37 us
    ppermute x4, waiting for transfers between devices, swap(): return lax.ppermute(array, 'core', [(0, 1), (1, 0)])  5.92 us
    ppermute x4, starting transfers between devices, swap(): return lax.ppermute(array, 'core', [(0, 1), (1, 0)])  3.72 us
  transfers between devices with their start and end apart: 4, of which 2 were waited for; matrix products, arithmetic and copies ran while one was open for 2% of the time, Pallas kernels for 53%

profile of v1, /device:TPU:1, one launch (start us, length us, event | category | flops | bytes accessed | tf_op | source)
XLA Modules:
  0.0 159.9 jit_solution(6728372720799944945)
XLA Ops:
  0.6 0.0 copy-start
  0.6 0.0 copy-start.6
  0.7 1.5 dynamic-slice_bitcast_fusion.2
  2.2 0.5 copy-done.6
  2.7 1.5 dynamic-slice_bitcast_fusion
  4.2 0.0 copy-start.7
  4.2 2.0 %pad_maximum_fusion = bf16[3,576,1024]{2,1,0:T(8,128)(2,1)} fusion(bf16[1,576,1024]{2,1,0:T(8,128)(2,1)S(1)} %get-tuple-element.23, bf16[1,576,1024]{2,1,0:T(8,128)(2,1)S(1)} %get-tuple-element.24, bf16[1,576,1024]{2,1,0:T(8,128)(2,1)S(1)} %dynamic-slice_bitcast_fusion.2), kind=kLoop, calls=%fused_computation | loop fusion | flops 3538944 | bytes 7077888 | tf_op jit(solution)/shard_map/stack | solution.py:391
  6.3 0.1 collective-permute-start
  6.3 0.1 mul.46
  6.5 0.1 mul.49
  6.8 0.5 collective-permute-start.1
  7.3 0.1 constant_dynamic-slice_fusion.2
  7.4 0.1 broadcast_in_dim.24
  7.5 0.1 tile.7
  7.6 0.1 broadcast_in_dim.25
  7.7 4.9 %collective-permute-done.1 = bf16[2,2,16,1024]{3,2,1,0:T(8,128)(2,1)S(1)} collective-permute-done((bf16[2,2,16,1024]{3,2,1,0:T(8,128)(2,1)S(1)}, bf16[2,2,16,1024]{3,2,1,0:T(8,128)(2,1)S(1)}, u32[]{:S(2)}, u32[]{:S(2)}) %collective-permute-start.1) | collective-permute-done | bytes 131104 | tf_op jit(solution)/shard_map/ppermute | solution.py:366
  12.7 0.7 fusion.5
  13.4 38.8 %shard_map.103 = (bf16[2,4,2,64,1024]{4,3,2,1,0:T(8,128)(2,1)}, bf16[2,4,2,64,1024]{4,3,2,1,0:T(8,128)(2,1)}) custom-call(bf16[64,1024]{1,0:T(8,128)(2,1)} %bitcast.45, bf16[64,1024]{1,0:T(8,128)(2,1)} %bitcast.44), custom_call_target="tpu_custom_call" | custom-call | tf_op jit(solution)/shard_map/pallas_call | solution.py:232
  52.2 0.1 broadcast_in_dim.26.bias_ref
  52.4 1.6 copy-done.4
  53.9 1.6 copy-done.5
  55.5 48.5 %shard_map.104 = (bf16[576,1024]{1,0:T(8,128)(2,1)S(1)}, bf16[576,1024]{1,0:T(8,128)(2,1)}, bf16[1024,1024]{1,0:T(8,128)(2,1)S(1)}, bf16[1024,1024]{1,0:T(8,128)(2,1)S(1)}) custom-call(s32[1]{0:T(128)} %bitcast.core_ref, f32[2,8,2,1,1152]{4,3,2,1,0:T(1,128)S(1)} %broadcast_in_dim.26.bias_ref, bf16[576,2048]{1,0:T(8,128)(2,1)S(1)} %bitcast.35, ...), custom_call_target="tpu_custom_call" | custom-call | flops 12079595520 | bytes 16646144 | tf_op jit(solution)/shard_map/pallas_call | solution.py:76
  104.0 1.3 copy-done.1
  105.3 1.3 copy-done.2
  106.7 1.3 collective-permute-start.2
  108.0 45.3 %shard_map.105 = bf16[2,64,1024]{2,1,0:T(8,128)(2,1)} custom-call(bf16[2,4,2,64,1024]{4,3,2,1,0:T(8,128)(2,1)} %bitcast.31, bf16[2,4,2,64,1024]{4,3,2,1,0:T(8,128)(2,1)} %bitcast.32), custom_call_target="tpu_custom_call" | custom-call | tf_op jit(solution)/shard_map/pallas_call | solution.py:334
  153.3 1.0 constant_dynamic-slice_fusion.1
  154.3 1.9 %collective-permute-start.3 = (bf16[2,2,16,1024]{3,2,1,0:T(8,128)(2,1)S(1)}, bf16[2,2,16,1024]{3,2,1,0:T(8,128)(2,1)S(1)}, u32[]{:S(2)}, u32[]{:S(2)}) collective-permute-start(bf16[2,2,16,1024]{3,2,1,0:T(8,128)(2,1)S(1)} %get-tuple-element.18), channel_id=1, source_target_pairs={{0,1},{1,0},{2,3},{3,2},{4,5},{5,4},{6,7},{7,6},{8,9},{9,8},{10,11... | collective-permute-start | bytes 393224 | tf_op jit(solution)/shard_map/ppermute | solution.py:366
  156.1 1.0 collective-permute-done.3
  157.1 0.1 maximum_select_fusion.2
  157.2 0.7 slice_bitcast_fusion
  157.9 1.9 %maximum_select_fusion = bf16[36,16,2048]{2,1,0:T(8,128)(2,1)} fusion(bf16[36,16,1024]{2,1,0:T(8,128)(2,1)S(1)} %bitcast.38, bf16[36,16,1024]{2,1,0:T(8,128)(2,1)S(1)} %bitcast.33, pred[]{:T(512)S(6)} %eq.8), kind=kLoop, calls=%fused_computation.1 | loop fusion | flops 10616832 | bytes 4718593 | tf_op jit(solution)/shard_map/jit(_where)/select_n | solution.py:370
  (24 shorter events, 0.3 us)
Async XLA Ops:
  0.6 6.7 %copy-start = (s32[72,2]{0,1:T(2,128)S(1)}, s32[72,2]{0,1:T(2,128)}, u32[]{:S(2)}) copy-start(s32[72,2]{0,1:T(2,128)} %param.15) | copy-start | bytes 1732
  0.6 2.0 %copy-start.6 = (bf16[36,16,2048]{2,1,0:T(8,128)(2,1)S(1)}, bf16[36,16,2048]{2,1,0:T(8,128)(2,1)}, u32[]{:S(2)}) copy-start(bf16[36,16,2048]{2,1,0:T(8,128)(2,1)} %param.9) | copy-start | bytes 7077892
  4.2 2.1 %copy-start.9 = (bf16[2,16,16]{2,1,0:T(8,128)(2,1)S(1)}, bf16[2,16,16]{2,1,0:T(8,128)(2,1)}, u32[]{:S(2)}) copy-start(bf16[2,16,16]{2,1,0:T(8,128)(2,1)} %param.12) | copy-start | bytes 3076
  4.2 2.3 %copy-start.10 = (bf16[2,16,16]{2,1,0:T(8,128)(2,1)S(1)}, bf16[2,16,16]{2,1,0:T(8,128)(2,1)}, u32[]{:S(2)}) copy-start(bf16[2,16,16]{2,1,0:T(8,128)(2,1)} %param.14) | copy-start | bytes 3076
  4.2 2.5 %copy-start.7 = (bf16[2,16,2048]{2,1,0:T(8,128)(2,1)S(1)}, bf16[2,16,2048]{2,1,0:T(8,128)(2,1)}, u32[]{:S(2)}) copy-start(bf16[2,16,2048]{2,1,0:T(8,128)(2,1)} %param.11) | copy-start | bytes 393220
  4.2 2.5 %copy-start.8 = (bf16[2,16,2048]{2,1,0:T(8,128)(2,1)S(1)}, bf16[2,16,2048]{2,1,0:T(8,128)(2,1)}, u32[]{:S(2)}) copy-start(bf16[2,16,2048]{2,1,0:T(8,128)(2,1)} %param.13) | copy-start | bytes 393220
  6.3 46.0 %collective-permute-start = (bf16[3,576,1024]{2,1,0:T(8,128)(2,1)}, bf16[3,576,1024]{2,1,0:T(8,128)(2,1)}, u32[]{:S(2)}, u32[]{:S(2)}) collective-permute-start(bf16[3,576,1024]{2,1,0:T(8,128)(2,1)} %pad_maximum_fusion), channel_id=1, source_target_pairs={{0,1},{1,0},{2,3},{3,2},{4,5},{5,4},{6,7},{7,6},{8,9},{9,8},{10,11... | collective-permute-start | bytes 10616840 | tf_op jit(solution)/shard_map/ppermute | solution.py:366
  6.4 45.9 %copy-start.3 = (bf16[36,16,2048]{2,1,0:T(8,128)(2,1)S(1)}, bf16[36,16,2048]{2,1,0:T(8,128)(2,1)}, u32[]{:S(2)}) copy-start(bf16[36,16,2048]{2,1,0:T(8,128)(2,1)} %param.8) | copy-start | bytes 7077892
  6.8 5.8 %collective-permute-start.1 = (bf16[2,2,16,1024]{3,2,1,0:T(8,128)(2,1)S(1)}, bf16[2,2,16,1024]{3,2,1,0:T(8,128)(2,1)S(1)}, u32[]{:S(2)}, u32[]{:S(2)}) collective-permute-start(bf16[2,2,16,1024]{3,2,1,0:T(8,128)(2,1)S(1)} %get-tuple-element.22), channel_id=1, source_target_pairs={{0,1},{1,0},{2,3},{3,2},{4,5},{5,4},{6,7},{7,6},{8,9},{9,8},{10,11... | collective-permute-start | bytes 393224 | tf_op jit(solution)/shard_map/ppermute | solution.py:366
  52.3 1.6 copy-start.4
  53.9 1.6 copy-start.5
  104.0 1.3 copy-start.1
  105.3 1.3 copy-start.2
  106.7 51.2 %collective-permute-start.2 = (bf16[576,1024]{1,0:T(8,128)(2,1)}, bf16[576,1024]{1,0:T(8,128)(2,1)S(1)}, u32[]{:S(2)}, u32[]{:S(2)}) collective-permute-start(bf16[576,1024]{1,0:T(8,128)(2,1)} %get-tuple-element.12), channel_id=1, source_target_pairs={{0,1},{1,0},{2,3},{3,2},{4,5},{5,4},{6,7},{7,6},{8,9},{9,8},{10,11... | collective-permute-start | bytes 3538952 | tf_op jit(solution)/shard_map/ppermute | solution.py:366
  154.3 2.8 %collective-permute-start.3 = (bf16[2,2,16,1024]{3,2,1,0:T(8,128)(2,1)S(1)}, bf16[2,2,16,1024]{3,2,1,0:T(8,128)(2,1)S(1)}, u32[]{:S(2)}, u32[]{:S(2)}) collective-permute-start(bf16[2,2,16,1024]{3,2,1,0:T(8,128)(2,1)S(1)} %get-tuple-element.18), channel_id=1, source_target_pairs={{0,1},{1,0},{2,3},{3,2},{4,5},{5,4},{6,7},{7,6},{8,9},{9,8},{10,11... | collective-permute-start | bytes 393224 | tf_op jit(solution)/shard_map/ppermute | solution.py:366

commit v2 on v1

v2 whole, which is shorter than its diff:
```python
import functools
import math

import jax
import jax.numpy as jnp
from jax import lax
from jax.experimental import pallas as pl
from jax.experimental.pallas import tpu as pltpu
from jax.sharding import Mesh, PartitionSpec as P

HD = 128
SCALE = HD ** -0.5
ROWS = 256
NT = (((1,), (1,)), ((), ()))
NN = (((1,), (0,)), ((), ()))


def dot(a, b, dims):
    return lax.dot_general(a, b, dims, preferred_element_type=jnp.float32)


MESH = pl.DeviceIdType.MESH


def place():
    group, chip, core = (lax.axis_index(name) for name in ("grp", "chip", "core"))
    line, pair = chip // 2, chip % 2
    beside = ((1 - group, chip, core), (group, line * 2 + 1 - pair, core))
    return group, line, pair, beside, lambda at: (group, at * 2 + pair, core)


def meet(lines, line, beside, along):
    barrier = pltpu.get_barrier_semaphore()
    for device in beside:
        pl.semaphore_signal(barrier, inc=1, device_id=device, device_id_type=MESH)
    for side in (-1, 1):
        @pl.when((line + side >= 0) & (line + side < lines))
        def _():
            pl.semaphore_signal(barrier, inc=1, device_id=along(line + side), device_id_type=MESH)
    count = 2 + (line > 0).astype(jnp.int32) + (line < lines - 1).astype(jnp.int32)
    pl.semaphore_wait(barrier, count)


def remote(src, dst, send, recv, device):
    return pltpu.make_async_remote_copy(
        src_ref=src, dst_ref=dst, send_sem=send, recv_sem=recv, device_id=device, device_id_type=MESH
    )


def each(lines, line, distance, body):
    for side in ((-1, 1) if distance else (0,)):
        at = line + side * distance
        if distance:
            @pl.when((at >= 0) & (at < lines))
            def _():
                body(side, at)
        else:
            body(side, at)


def gather_steps(
    lines, k_in, v_in, k_out, v_out,
    local_sem, z_send, z_recv, s_send, s_recv, f_send, f_recv,
):
    group, line, pair, beside, along = place()
    ins, outs = (k_in, v_in), (k_out, v_out)
    locals_ = [
        pltpu.make_async_copy(ins[kind], outs[kind].at[group, line, pair], local_sem.at[kind])
        for kind in range(2)
    ]

    def begin():
        for copy in locals_:
            copy.start()
        meet(lines, line, beside, along)

    def relay(kind, side, at, first):
        slot = outs[kind].at[group, at, pair]
        way = (side + 1) // 2
        return remote(
            ins[kind] if first else slot, slot, z_send.at[kind, way, at], z_recv.at[kind, at],
            along(line + side),
        )

    def sideways(kind, way, at, first):
        slot = outs[kind].at[group, at, pair]
        return remote(
            ins[kind] if first else slot, slot, s_send.at[kind, way, at], s_recv.at[kind, way, at],
            beside[way],
        )

    def forward(kind, at):
        slot = outs[0].at[1 - group, at, pair] if kind == 0 else outs[1].at[group, at, 1 - pair]
        return remote(slot, slot, f_send.at[kind, at], f_recv.at[kind, at], beside[1 - kind])

    def spread(distance):
        def body(side, at):
            for kind in range(2):
                if distance:
                    relay(kind, side, at, False).wait_recv()
                for onward in ((-1, 1) if distance == 0 else (-side,)):
                    @pl.when((line + onward >= 0) & (line + onward < lines))
                    def _():
                        relay(kind, onward, at, distance == 0).start()
                for way in (kind, 1 - kind):
                    sideways(kind, way, at, distance == 0).start()
        each(lines, line, distance, body)

    def across(distance):
        def body(side, at):
            for kind in range(2):
                sideways(kind, kind, at, False).wait_recv()
                forward(kind, at).start()
        each(lines, line, distance, body)

    def finish(distance):
        def body(side, at):
            for kind in range(2):
                sideways(kind, 1 - kind, at, False).wait_recv()
                forward(kind, at).wait_recv()
                forward(kind, at).wait_send()
                for way in range(2):
                    sideways(kind, way, at, False).wait_send()
                for onward in ((-1, 1) if distance == 0 else (-side,)):
                    @pl.when((line + onward >= 0) & (line + onward < lines))
                    def _():
                        relay(kind, onward, at, False).wait_send()
        each(lines, line, distance, body)

    def end():
        for distance in range(lines):
            finish(distance)
        for copy in locals_:
            copy.wait()

    def turn(distance):
        if distance == 0:
            begin()
        if distance < lines:
            spread(distance)
        if distance:
            across(distance - 1)

    turns = [functools.partial(turn, distance) for distance in range(lines + 1)]
    return turns, end


def run(steps):
    turns, end = steps
    for turn in turns:
        turn()
    end()


def gather_kernel(lines, *refs):
    run(gather_steps(lines, *refs))


def gather_scratch(lines):
    dma = pltpu.SemaphoreType.DMA
    return [
        dma((2,)), dma((2, 2, lines)), dma((2, lines)), dma((2, 2, lines)), dma((2, 2, lines)),
        dma((2, lines)), dma((2, lines)),
    ]


def gather(keys, values, lines):
    shape = jax.ShapeDtypeStruct((2, lines, 2) + keys.shape, keys.dtype)
    anywhere = pl.BlockSpec(memory_space=pl.ANY)
    return pl.pallas_call(
        functools.partial(gather_kernel, lines),
        in_specs=[anywhere] * 2,
        out_specs=[anywhere] * 2,
        out_shape=[shape] * 2,
        scratch_shapes=gather_scratch(lines),
        compiler_params=pltpu.CompilerParams(collective_id=0, has_side_effects=True),
        cost_estimate=pl.CostEstimate(flops=0, bytes_accessed=2 ** 26, transcendentals=0),
    )(keys, values)


def scatter_steps(
    lines, k_ref, v_ref, out_ref, first_in, second_out, second_in, line_out, line_in, total,
    a_send, a_recv, b_send, b_recv, z_send, z_recv,
):
    group, line, pair, beside, along = place()
    refs = (k_ref, v_ref)

    def first(kind, at):
        src = k_ref.at[1 - group, at] if kind == 0 else v_ref.at[:, at, 1 - pair]
        return remote(src, first_in.at[kind, at], a_send.at[kind, at], a_recv.at[kind, at], beside[kind])

    def second(kind, at):
        return remote(
            second_out.at[kind, at], second_in.at[kind, at], b_send.at[kind, at], b_recv.at[kind, at],
            beside[1 - kind],
        )

    def pass_on(kind, side, at):
        way = (side + 1) // 2
        return remote(
            line_out.at[kind, at], line_in.at[kind, way, at], z_send.at[kind, at],
            z_recv.at[kind, way, at], along(line + side),
        )

    def start(distance):
        def body(side, at):
            for kind in range(2):
                first(kind, at).start()
        each(lines, line, distance, body)

    def halve(distance):
        def body(side, at):
            for kind in range(2):
                first(kind, at).wait_recv()
                if kind == 0:
                    mine, come = k_ref[group, at, 1 - pair], first_in[0, at, 1 - pair]
                else:
                    mine, come = v_ref[1 - group, at, pair], first_in[1, at, 1 - group]
                second_out[kind, at] = (mine.astype(jnp.float32) + come.astype(jnp.float32)).astype(jnp.bfloat16)
                second(kind, at).start()
        each(lines, line, distance, body)

    def collect(distance):
        def body(side, at):
            for kind in range(2):
                second(kind, at).wait_recv()
                come = first_in[kind, at, pair if kind == 0 else group]
                total[kind] = (
                    refs[kind][group, at, pair].astype(jnp.float32) + come.astype(jnp.float32)
                    + second_in[kind, at].astype(jnp.float32)
                )
                for way in ((-1, 1) if distance == 0 else (side,)):
                    @pl.when((line - way >= 0) & (line - way < lines))
                    def _():
                        pass_on(kind, way, at).wait_recv()
                        total[kind] += line_in[kind, (way + 1) // 2, at].astype(jnp.float32)
                if distance:
                    line_out[kind, at] = total[kind].astype(jnp.bfloat16)
                    pass_on(kind, side, at).start()
                else:
                    out_ref[kind] = total[kind].astype(jnp.bfloat16)
        each(lines, line, distance, body)

    def finish(distance):
        def body(side, at):
            for kind in range(2):
                first(kind, at).wait_send()
                second(kind, at).wait_send()
                if distance:
                    pass_on(kind, side, at).wait_send()
        each(lines, line, distance, body)

    order = list(range(lines - 1, -1, -1))

    def turn(count):
        if count == 0:
            meet(lines, line, beside, along)
        if count < lines:
            start(order[count])
        if 0 <= count - 2 < lines:
            halve(order[count - 2])
        if 0 <= count - 3 < lines:
            collect(order[count - 3])

    def end():
        for distance in range(lines):
            finish(distance)

    return [functools.partial(turn, count) for count in range(lines + 3)], end


def scatter_kernel(lines, *refs):
    run(scatter_steps(lines, *refs))


def scatter_scratch(lines, rows, width):
    dma = pltpu.SemaphoreType.DMA
    return [
        pltpu.VMEM((2, lines, 2, rows, width), jnp.bfloat16),
        pltpu.VMEM((2, lines, rows, width), jnp.bfloat16),
        pltpu.VMEM((2, lines, rows, width), jnp.bfloat16),
        pltpu.VMEM((2, lines, rows, width), jnp.bfloat16),
        pltpu.VMEM((2, 2, lines, rows, width), jnp.bfloat16),
        pltpu.VMEM((2, rows, width), jnp.float32),
        dma((2, lines)), dma((2, lines)), dma((2, lines)), dma((2, lines)),
        dma((2, lines)), dma((2, 2, lines)),
    ]


def scatter(dk, dv):
    lines, rows, half = dk.shape[1], dk.shape[3], dk.shape[4]
    here = pl.BlockSpec(memory_space=pltpu.VMEM)
    return pl.pallas_call(
        functools.partial(scatter_kernel, lines),
        in_specs=[here] * 2,
        out_specs=here,
        out_shape=jax.ShapeDtypeStruct((2, rows, half), jnp.bfloat16),
        scratch_shapes=scatter_scratch(lines, rows, half),
        compiler_params=pltpu.CompilerParams(
            collective_id=3, has_side_effects=True, vmem_limit_bytes=56 * 2 ** 20,
        ),
        cost_estimate=pl.CostEstimate(flops=0, bytes_accessed=2 ** 26, transcendentals=0),
    )(dk, dv)


def grads_body(
    refs, outs, scratch, tick,
):
    bias_ref, q_own, g_own, o_own, swapped, k_ref, v_ref = refs
    dq_own, dq_in, dk_ref, dv_ref = outs
    q_all, g_all, dots, dq_all, dk_acc, dv_acc = scratch
    own = q_own.shape[0]
    rows = 2 * own
    keys = k_ref.shape[0]
    q_all[:own] = q_own[...]
    q_all[own:] = swapped[0]
    g_all[:own] = g_own[...]
    g_all[own:] = swapped[1]
    ones = jnp.ones((8, HD), jnp.bfloat16)
    for part, (grad, out) in enumerate(((g_own[...], o_own[...]), (swapped[1], swapped[2]))):
        product = grad.astype(jnp.float32) * out.astype(jnp.float32)
        high = product.astype(jnp.bfloat16)
        low = (product - high.astype(jnp.float32)).astype(jnp.bfloat16)
        dots[:, part * own:(part + 1) * own] = dot(ones, high, NT) + dot(ones, low, NT)
    k_all = k_ref[...]
    v_all = v_ref[...]
    k_turned = k_all.astype(jnp.float32).T.astype(jnp.bfloat16)
    dk_acc[...] = jnp.zeros_like(dk_acc)
    dv_acc[...] = jnp.zeros_like(dv_acc)
    for index, start in enumerate(range(0, rows, ROWS)):
        tick(index)
        size = min(ROWS, rows - start)
        at = pl.ds(start, size)
        q = q_all[at, :]
        g = g_all[at, :]
        bias = bias_ref[:, :, :, :, at]
        scores = dot(k_all, q, NT)
        span = keys // (bias.shape[0] * bias.shape[1] * bias.shape[2])
        masked = scores.reshape(bias.shape[:3] + (span, size)) + bias
        masked = masked.reshape(keys, size)
        highest = jnp.max(masked, axis=0, keepdims=True)
        weights = jnp.exp2((masked - highest) * (SCALE * math.log2(math.e)))
        probs = weights * (1.0 / jnp.sum(weights, axis=0, keepdims=True))
        dv_acc[...] += dot(probs.astype(jnp.bfloat16), g, NN)
        prob_grad = dot(v_all, g, NT)
        score_grad = (probs * (prob_grad - dots[0:1, at]) * SCALE).astype(jnp.bfloat16)
        dk_acc[...] += dot(score_grad, q, NN)
        dq_all[at, :] = dot(k_turned, score_grad, NN).T.astype(jnp.bfloat16)
    dq_own[...] = dq_all[:own]
    dq_in[...] = dq_all[own:]
    dk_ref[...] = dk_acc[...].astype(jnp.bfloat16)
    dv_ref[...] = dv_acc[...].astype(jnp.bfloat16)


def grads_kernel(lines, heads, steps, moved_out, *refs):
    ins, rest = refs[:7], refs[7:]
    moved, rest = rest[:2], rest[2:]
    outs, rest = rest[:4], rest[4:]
    arrived, rest = rest[:moved_out], rest[moved_out:]
    scratch, extra = rest[:6], rest[6:]
    turns, end = steps(lines, *moved, *arrived, *extra)
    per_head = pl.cdiv(2 * ins[1].shape[0], ROWS)
    slots = per_head * heads
    head = pl.program_id(0)

    def tick(index):
        for count, turn in enumerate(turns):
            slot = count * slots // len(turns)
            if slot % per_head == index:
                pl.when(head == slot // per_head)(turn)

    grads_body(ins, outs, scratch, tick)
    pl.when(head == heads - 1)(end)


def local_grads(part, parts, lines, bias, q, g, o, swapped, keys, values, moved, gathering):
    own, half = q.shape[0], q.shape[1] // 2
    heads = half // HD // parts
    count, width = keys.shape[0], heads * HD
    first = part * heads
    mine = pl.BlockSpec((own, HD), lambda h: (0, lax.axis_index("core") * (heads * parts) + first + h))
    column = pl.BlockSpec((own, HD), lambda h: (0, h))
    table = pl.BlockSpec((count, HD), lambda h: (0, h))
    anywhere = pl.BlockSpec(memory_space=pl.ANY)
    here = pl.BlockSpec(memory_space=pltpu.VMEM)
    if gathering:
        steps, specs, extra_specs = gather_steps, [anywhere] * 2, [anywhere] * 2
        extra = [jax.ShapeDtypeStruct((2, lines, 2) + moved[0].shape, jnp.bfloat16)] * 2
        more = gather_scratch(lines)
    else:
        rows = moved[0].shape[3]
        steps, specs, extra_specs = scatter_steps, [here] * 2, [here]
        extra = [jax.ShapeDtypeStruct((2, rows, width), jnp.bfloat16)]
        more = scatter_scratch(lines, rows, width)
    return pl.pallas_call(
        functools.partial(grads_kernel, lines, heads, steps, len(extra)),
        grid=(heads,),
        in_specs=[
            pl.BlockSpec(bias.shape, lambda h: (0, 0, 0, 0, 0)),
            mine, mine, mine,
            pl.BlockSpec((3, own, HD), lambda h: (0, 0, first + h)),
            table, table,
        ] + specs,
        out_specs=[column, column, table, table] + extra_specs,
        scratch_shapes=[
            pltpu.VMEM((2 * own, HD), jnp.bfloat16),
            pltpu.VMEM((2 * own, HD), jnp.bfloat16),
            pltpu.VMEM((8, 2 * own), jnp.float32),
            pltpu.VMEM((2 * own, HD), jnp.bfloat16),
            pltpu.VMEM((count, HD), jnp.float32),
            pltpu.VMEM((count, HD), jnp.float32),
        ] + more,
        out_shape=[
            jax.ShapeDtypeStruct((own, width), jnp.bfloat16),
            jax.ShapeDtypeStruct((own, width), jnp.bfloat16),
            jax.ShapeDtypeStruct((count, width), jnp.bfloat16),
            jax.ShapeDtypeStruct((count, width), jnp.bfloat16),
        ] + extra,
        compiler_params=pltpu.CompilerParams(
            collective_id=1 if gathering else 2, has_side_effects=True,
            vmem_limit_bytes=56 * 2 ** 20,
        ),
        cost_estimate=pl.CostEstimate(
            flops=20 * own * count * width, bytes_accessed=14 * own * width + 8 * count * width,
            transcendentals=2 * own * count * heads,
        ),
    )(bias, q, g, o, swapped, keys, values, *moved)


def dequantize(codes, scales):
    count, length, width = codes.shape
    heads = scales.shape[2]
    values = (
        codes.astype(jnp.float32).reshape(count, length, heads, width // heads)
        * scales.astype(jnp.float32)[..., None]
    )
    return values.reshape(count, length, width).astype(jnp.bfloat16)


def swap(array):
    return lax.ppermute(array, "core", [(0, 1), (1, 0)])


def in_order(core, mine, other, axis):
    return jnp.where(
        core == 0,
        jnp.concatenate([mine, other], axis=axis),
        jnp.concatenate([other, mine], axis=axis),
    )


def on_device(group_count, lines, query, out_grad, forward_out, key_codes, key_scale, value_codes, value_scale, pairing):
    core = lax.axis_index("core")
    group = lax.axis_index("grp")
    blocks, tokens, width = query.shape
    half = width // 2
    own = blocks * tokens
    table = jnp.stack([dequantize(key_codes, key_scale), dequantize(value_codes, value_scale)])
    kept = lax.dynamic_slice_in_dim(table, core * half, half, axis=3)
    other = swap(lax.dynamic_slice_in_dim(table, (1 - core) * half, half, axis=3))
    shard = in_order(core, kept, other, 2)
    kv_local, kv_tokens = shard.shape[1:3]
    shard = shard.reshape(2, kv_local * kv_tokens, half)
    shards = [(shard[0, :, at:at + half // 2], shard[1, :, at:at + half // 2]) for at in (0, half // 2)]
    near = [a.reshape(-1, half // 2) for a in gather(*shards[0], lines)]
    flat = [a.reshape(own, width) for a in (query, out_grad, forward_out)]
    swapped = swap(jnp.stack([
        lax.dynamic_slice_in_dim(a, (1 - core) * half, half, axis=1) for a in flat
    ]))
    chips = near[0].shape[0] // (group_count * kv_local * kv_tokens)
    chosen = lax.dynamic_slice_in_dim(pairing, group * blocks, blocks, axis=0)
    hit = jnp.any(chosen[None] == jnp.arange(group_count * kv_local)[:, None, None], axis=2)
    bias = jnp.where(hit, 0.0, -jnp.inf).astype(jnp.float32)
    bias = jnp.tile(jnp.repeat(bias, tokens, axis=1), (1, 2))
    bias = bias.reshape(group_count, 1, kv_local, 1, 2 * own)
    bias = jnp.broadcast_to(bias, (group_count, chips, kv_local, 1, 2 * own))
    split = (2, lines, 2, kv_local * kv_tokens, half // 2)
    mine_0, other_0, dk_0, dv_0, *far = local_grads(
        0, 2, lines, bias, *flat, swapped, *near, shards[1], True
    )
    far = [a.reshape(-1, half // 2) for a in far]
    mine_1, other_1, dk_1, dv_1, sums_0 = local_grads(
        1, 2, lines, bias, *flat, swapped, *far, (dk_0.reshape(split), dv_0.reshape(split)), False
    )
    sums_1 = scatter(dk_1.reshape(split), dv_1.reshape(split))
    dq = in_order(
        core, jnp.concatenate([mine_0, mine_1], axis=1),
        jnp.concatenate([swap(other_0), swap(other_1)], axis=1), 1,
    ).reshape(query.shape)
    sums = jnp.concatenate([sums_0, sums_1], axis=2).reshape(2, kv_local, kv_tokens, half)
    length = kv_tokens // 2
    kept = lax.dynamic_slice_in_dim(sums, core * length, length, axis=2)
    other = swap(lax.dynamic_slice_in_dim(sums, (1 - core) * length, length, axis=2))
    grads = in_order(core, kept, other, 3)
    return dq, grads[0], grads[1]


def solution(mesh):
    groups, heads = mesh.shape["grp"], mesh.shape["head"]
    split = Mesh(mesh.devices.reshape(groups, heads // 2, 2), ("grp", "chip", "core"))
    spec = P("grp", ("chip", "core"), None)
    return jax.shard_map(
        functools.partial(on_device, groups, heads // 4),
        mesh=split,
        in_specs=(spec,) * 7 + (P(),),
        out_specs=(spec,) * 3,
        check_vma=False,
    )
```

time: 161 us -> 151 us (0.938)
  Pallas kernels: 133 us -> 114 us
  starting transfers between devices: 3.72 us -> 11.9 us
  waiting for transfers between devices: 5.92 us -> 1.54 us
  local copies, waits for them, and re-layouts: 12.6 us -> 16.2 us
  other arithmetic: 4.18 us -> 6.45 us
    pallas_call x1, Pallas kernels: 45.3 us -> 20.2 us  [scatter(): pl.pallas_call(functools.partial(scatter_kernel, lines), in_specs=[here]...]
    pallas_call x1 -> x2, Pallas kernels: 48.5 us -> 70.4 us  [local_grads(): pl.pallas_call(functools.partial(grads_kernel, lines, heads, steps, len(e...]
    pallas_call x1, Pallas kernels: 38.8 us -> 23.5 us  [gather(): pl.pallas_call(functools.partial(gather_kernel, lines), in_specs=[anywher...]
    ppermute x4 -> x5, starting transfers between devices: 3.72 us -> 11.9 us  [swap(): return lax.ppermute(array, 'core', [(0, 1), (1, 0)])]
    unnamed x22 -> x14, local copies, waits for them, and re-layouts: 6.37 us -> 0.65 us
    mul x4, local copies, waits for them, and re-layouts: 0.34 us -> 5.76 us  [dequantize(): codes.astype(jnp.float32).reshape(count, length, heads, width // heads)]
    ppermute x4 -> x5, waiting for transfers between devices: 5.92 us -> 1.54 us  [swap(): return lax.ppermute(array, 'core', [(0, 1), (1, 0)])]
    broadcast_in_dim x2, local copies, waits for them, and re-layouts: 0.18 us -> 2.88 us  [on_device(): bias = jnp.broadcast_to(bias, (group_count, chips, kv_local, 1, 2 * own))]
  transfers between devices with their start and end apart: 4 -> 5, of which waited for: 2 -> 3; matrix products, arithmetic and copies ran while one was open for 2% -> 9% of each run, Pallas kernels for 53% -> 16%
where the time goes in v2:
time: 151 us
  Pallas kernels  114 us (75%)
  local copies, waits for them, and re-layouts  16.2 us (11%)
  starting transfers between devices  11.9 us (8%)
  other arithmetic  6.45 us (4%)
  waiting for transfers between devices  1.54 us (1%)
    pallas_call x2, Pallas kernels, local_grads(): pl.pallas_call(functools.partial(grads_kernel, lines, heads, steps, len(e...  70.4 us
    pallas_call x1, Pallas kernels, gather(): pl.pallas_call(functools.partial(gather_kernel, lines), in_specs=[anywher...  23.5 us
    pallas_call x1, Pallas kernels, scatter(): pl.pallas_call(functools.partial(scatter_kernel, lines), in_specs=[here]...  20.2 us
    ppermute x5, starting transfers between devices, swap(): return lax.ppermute(array, 'core', [(0, 1), (1, 0)])  11.9 us
    mul x4, local copies, waits for them, and re-layouts, dequantize(): codes.astype(jnp.float32).reshape(count, length, heads, width // heads)  5.76 us
    select_n x3, other arithmetic, in_order(): jnp.where(core == 0, jnp.concatenate([mine, other], axis=axis), jnp.conca...  3.1 us
    another operation x2, local copies, waits for them, and re-layouts, on_device(): jnp.stack([lax.dynamic_slice_in_dim(a, (1 - core) * half, half, axis=1) f...  3.08 us
  transfers between devices with their start and end apart: 5, of which 3 were waited for; matrix products, arithmetic and copies ran while one was open for 9% of the time, Pallas kernels for 16%

profile of v2, /device:TPU:1, one launch (start us, length us, event | category | flops | bytes accessed | tf_op | source)
XLA Modules:
  0.0 150.9 jit_solution(7423910565852121090)
XLA Ops:
  0.7 1.5 dynamic-slice_bitcast_fusion.2
  2.2 0.5 copy-done.3
  2.7 1.6 %dynamic-slice_bitcast_fusion = (bf16[1,576,1024]{2,1,0:T(8,128)(2,1)S(1)}, bf16[1,576,1024]{2,1,0:T(8,128)(2,1)S(1)}) fusion(bf16[576,2048]{1,0:T(8,128)(2,1)} %bitcast.54, s32[]{:T(128)S(6)} %select_n.54, bf16[576,2048]{1,0:T(8,128)(2,1)S(1)} %bitcast.53), kind=kLoop, calls=%fused_computation.2 | loop fusion | bytes 4718596 | tf_op jit(solution)/shard_map/stack | solution.py:467
  4.3 0.4 pad_maximum_fusion
  4.7 0.1 collective-permute-start
  4.8 0.1 copy-done.4
  4.9 0.8 mul.42
  5.8 1.7 %mul.43 = f32[2,16,2048]{2,1,0:T(8,128)} reshape(f32[2,16,16,128]{3,2,1,0:T(8,128)} %mul.42) | data formatting | bytes 524288 | tf_op jit(solution)/shard_map/mul | solution.py:434
  7.5 1.5 %mul.45 = f32[2,16,16,128]{3,2,1,0:T(8,128)} broadcast(bf16[2,16,16]{2,1,0:T(8,128)(2,1)} %param.14), dimensions={0,1,2} | broadcast | bytes 263168 | tf_op jit(solution)/shard_map/mul | solution.py:434
  9.0 1.7 %mul.46 = f32[2,16,2048]{2,1,0:T(8,128)} reshape(f32[2,16,16,128]{3,2,1,0:T(8,128)} %mul.45) | data formatting | bytes 524288 | tf_op jit(solution)/shard_map/mul | solution.py:434
  10.7 1.2 fusion
  11.9 0.7 fusion.3
  12.6 0.3 collective-permute-start.1
  13.0 0.7 broadcast_in_dim.24
  13.8 1.0 tile.7
  14.8 0.6 tile.8
  15.4 1.4 broadcast_in_dim.25
  16.8 1.2 maximum_select_fusion.1
  18.0 0.7 slice_bitcast_fusion.2
  18.7 23.5 %shard_map.103 = (bf16[2,4,2,64,512]{4,3,2,1,0:T(8,128)(2,1)}, bf16[2,4,2,64,512]{4,3,2,1,0:T(8,128)(2,1)}) custom-call(bf16[64,512]{1,0:T(8,128)(2,1)} %get-tuple-element.36.refs_0_, bf16[64,512]{1,0:T(8,128)(2,1)} %get-tuple-element.35.refs_1_), custom_call_target="tpu_custom_call" | custom-call | bytes 67108864 | tf_op jit(solution)/shard_map/pallas_call | solution.py:170
  42.2 1.5 broadcast_in_dim.26.refs_0_
  43.6 34.2 %shard_map.104 = (bf16[576,512]{1,0:T(8,128)(2,1)}, bf16[576,512]{1,0:T(8,128)(2,1)}, bf16[1024,512]{1,0:T(8,128)(2,1)}, bf16[1024,512]{1,0:T(8,128)(2,1)}, bf16...) custom-call(f32[2,8,2,1,1152]{4,3,2,1,0:T(1,128)} %broadcast_in_dim.26.refs_0_, ...), custom_call_target="tpu_custom_call" | custom-call | flops 6039797760 | bytes 8323072 | tf_op jit(solution)/shard_map/pallas_call | solution.py:395
  77.8 36.2 %shard_map.105 = (bf16[576,512]{1,0:T(8,128)(2,1)}, bf16[576,512]{1,0:T(8,128)(2,1)}, bf16[1024,512]{1,0:T(8,128)(2,1)}, bf16[1024,512]{1,0:T(8,128)(2,1)}, bf16[2,64,512]{2,1,0:T(8,128)(2,1)}) custom-call(f32[2,8,2,1,1152]{4,3,2,1,0:T(1,128)} %broadcast_in_dim.26.refs_0_, bf16[576,2048]{1,0:T(8,128)(2,1)} %bitcast.59, bf16[576,2048]{1,0:T(8,128)(2,1)} %bitcast.52, ...), custom_call_target="tpu_custom_call" | custom-call | flops 6039797760 | bytes 8323072 | tf_op jit(solution)/shard_map/pallas_call | solution.py:395
  114.0 20.2 %shard_map.106 = bf16[2,64,512]{2,1,0:T(8,128)(2,1)} custom-call(bf16[2,4,2,64,512]{4,3,2,1,0:T(8,128)(2,1)} %bitcast.44, bf16[2,4,2,64,512]{4,3,2,1,0:T(8,128)(2,1)} %bitcast.45), custom_call_target="tpu_custom_call" | custom-call | bytes 67108864 | tf_op jit(solution)/shard_map/pallas_call | solution.py:293
  134.2 1.0 pad_maximum_fusion.1
  135.2 10.9 %collective-permute-start.4 = (bf16[2,2,16,1024]{3,2,1,0:T(8,128)(2,1)S(1)}, bf16[2,2,16,1024]{3,2,1,0:T(8,128)(2,1)S(1)}, u32[]{:S(2)}, u32[]{:S(2)}) collective-permute-start(bf16[2,2,16,1024]{3,2,1,0:T(8,128)(2,1)S(1)} %get-tuple-element.32), channel_id=1, source_target_pairs={{0,1},{1,0},{2,3},{3,2},{4,5},{5,4},{6,7},{7,6},{8,9},{9,8},{10,11... | collective-permute-start | bytes 393224 | tf_op jit(solution)/shard_map/ppermute | solution.py:441
  146.2 0.4 collective-permute-start.2
  146.7 0.5 collective-permute-done.4
  147.2 0.7 slice_bitcast_fusion
  147.9 0.2 collective-permute-done.3
  148.1 0.8 collective-permute-done.2
  149.0 1.9 %maximum_select_fusion = bf16[36,16,2048]{2,1,0:T(8,128)(2,1)} fusion(bf16[36,16,512]{2,1,0:T(8,128)(2,1)S(1)} %bitcast.49, bf16[36,16,512]{2,1,0:T(8,128)(2,1)S(1)} %bitcast.50, bf16[36,16,512]{2,1,0:T(8,128)(2,1)S(1)} %bitcast.48, bf16[36,16,512]{2,1,0:T(8,128)(2,1)S(1)} %bitcast.47, pred[]{:T(512)S(6)} %eq.8), kind=kLoop, calls=%fused_computation.1 | loop fusion | flops 20054016 | bytes 4718593 | tf_op jit(solution)/shard_map/jit(_where)/select_n | solution.py:445
  (20 shorter events, 0.3 us)
Async XLA Ops:
  0.6 12.3 %copy-start = (s32[72,2]{0,1:T(2,128)S(1)}, s32[72,2]{0,1:T(2,128)}, u32[]{:S(2)}) copy-start(s32[72,2]{0,1:T(2,128)} %param.15) | copy-start | bytes 1732
  0.6 2.0 %copy-start.3 = (bf16[36,16,2048]{2,1,0:T(8,128)(2,1)S(1)}, bf16[36,16,2048]{2,1,0:T(8,128)(2,1)}, u32[]{:S(2)}) copy-start(bf16[36,16,2048]{2,1,0:T(8,128)(2,1)} %param.9) | copy-start | bytes 7077892
  4.2 0.7 copy-start.4
  4.7 37.4 %collective-permute-start = (bf16[3,576,1024]{2,1,0:T(8,128)(2,1)S(1)}, bf16[3,576,1024]{2,1,0:T(8,128)(2,1)}, u32[]{:S(2)}, u32[]{:S(2)}) collective-permute-start(bf16[3,576,1024]{2,1,0:T(8,128)(2,1)S(1)} %pad_maximum_fusion), channel_id=1, source_target_pairs={{0,1},{1,0},{2,3},{3,2},{4,5},{5,4},{6,7},{7,6},{8,9},{9,8},{10,11... | collective-permute-start | bytes 10616840 | tf_op jit(solution)/shard_map/ppermute | solution.py:441
  12.6 4.2 %collective-permute-start.1 = (bf16[2,2,16,1024]{3,2,1,0:T(8,128)(2,1)}, bf16[2,2,16,1024]{3,2,1,0:T(8,128)(2,1)}, u32[]{:S(2)}, u32[]{:S(2)}) collective-permute-start(bf16[2,2,16,1024]{3,2,1,0:T(8,128)(2,1)} %get-tuple-element.38), channel_id=1, source_target_pairs={{0,1},{1,0},{2,3},{3,2},{4,5},{5,4},{6,7},{7,6},{8,9},{9,8},{10,11... | collective-permute-start | bytes 393224 | tf_op jit(solution)/shard_map/ppermute | solution.py:441
  114.0 32.1 %copy-start.6 = (bf16[576,512]{1,0:T(8,128)(2,1)S(1)}, bf16[576,512]{1,0:T(8,128)(2,1)}, u32[]{:S(2)}) copy-start(bf16[576,512]{1,0:T(8,128)(2,1)} %get-tuple-element.25) | copy-start | bytes 1769476
  114.0 32.2 %copy-start.5 = (bf16[576,512]{1,0:T(8,128)(2,1)S(1)}, bf16[576,512]{1,0:T(8,128)(2,1)}, u32[]{:S(2)}) copy-start(bf16[576,512]{1,0:T(8,128)(2,1)} %get-tuple-element.24) | copy-start | bytes 1769476
  114.0 35.0 %copy-start.1 = (bf16[576,512]{1,0:T(8,128)(2,1)S(1)}, bf16[576,512]{1,0:T(8,128)(2,1)}, u32[]{:S(2)}) copy-start(bf16[576,512]{1,0:T(8,128)(2,1)} %get-tuple-element.18) | copy-start | bytes 1769476
  114.0 35.0 %copy-start.2 = (bf16[576,512]{1,0:T(8,128)(2,1)S(1)}, bf16[576,512]{1,0:T(8,128)(2,1)}, u32[]{:S(2)}) copy-start(bf16[576,512]{1,0:T(8,128)(2,1)} %get-tuple-element.23) | copy-start | bytes 1769476
  135.2 11.9 %collective-permute-start.4 = (bf16[2,2,16,1024]{3,2,1,0:T(8,128)(2,1)S(1)}, bf16[2,2,16,1024]{3,2,1,0:T(8,128)(2,1)S(1)}, u32[]{:S(2)}, u32[]{:S(2)}) collective-permute-start(bf16[2,2,16,1024]{3,2,1,0:T(8,128)(2,1)S(1)} %get-tuple-element.32), channel_id=1, source_target_pairs={{0,1},{1,0},{2,3},{3,2},{4,5},{5,4},{6,7},{7,6},{8,9},{9,8},{10,11... | collective-permute-start | bytes 393224 | tf_op jit(solution)/shard_map/ppermute | solution.py:441
  146.1 2.0 %collective-permute-start.3 = (bf16[576,512]{1,0:T(8,128)(2,1)S(1)}, bf16[576,512]{1,0:T(8,128)(2,1)S(1)}, u32[]{:S(2)}, u32[]{:S(2)}) collective-permute-start(bf16[576,512]{1,0:T(8,128)(2,1)S(1)} %copy-done.6), channel_id=1, source_target_pairs={{0,1},{1,0},{2,3},{3,2},{4,5},{5,4},{6,7},{7,6},{8,9},{9,8},{10,11... | collective-permute-start | bytes 1769480 | tf_op jit(solution)/shard_map/ppermute | solution.py:441
  146.2 2.8 %collective-permute-start.2 = (bf16[576,512]{1,0:T(8,128)(2,1)S(1)}, bf16[576,512]{1,0:T(8,128)(2,1)S(1)}, u32[]{:S(2)}, u32[]{:S(2)}) collective-permute-start(bf16[576,512]{1,0:T(8,128)(2,1)S(1)} %copy-done.5), channel_id=1, source_target_pairs={{0,1},{1,0},{2,3},{3,2},{4,5},{5,4},{6,7},{7,6},{8,9},{9,8},{10,11... | collective-permute-start | bytes 1769480 | tf_op jit(solution)/shard_map/ppermute | solution.py:441
